TPU v7x, 256 devices: a whole 4x4x8 slice. The times are simulated.
256 devices in a mesh: dp: 32 (over y_hi, z, core), ctx: 8 (over y_lo, x).
Axes of the slice: x: 4, y: 4 (y_hi: 2, y_lo: 2; y = y_hi * 2 + y_lo), z: 8, core: 2. Of those that a mesh axis runs over, the one named last changes fastest.
Arguments:
- inputs: bfloat16 [64, 512, 1024], P('dp', 'ctx'), may hold values from -8 to 8
- frames: int32 [64], P('dp'), may hold values from 64 to 512, as said below
- gain_first: float32 [1024], replicated, may hold values from 0.25 to 1.75
- w_first: bfloat16 [1024, 2048], P('dp'), may hold values from -0.1875 to 0.1875
- depth_kernel: float32 [31, 1024], replicated, may hold values from -1 to 1
- gain_second: float32 [1024], replicated, may hold values from 0.25 to 1.75
- w_second: bfloat16 [1024, 1024], P('dp'), may hold values from -0.1875 to 0.1875
- gain_attn: float32 [1024], replicated, may hold values from 0.25 to 1.75
- w_qkv: bfloat16 [1024, 3072], P('dp'), may hold values from -2.25 to 2.25
- w_proj: bfloat16 [1024, 1024], P('dp'), may hold values from -2.5 to 2.5
- grad_out: bfloat16 [64, 512, 1024], P('dp', 'ctx'), may hold values from -6 to 6
Outputs:
- result: bfloat16 [64, 512, 1024], P('dp', 'ctx')
- grad_in: bfloat16 [64, 512, 1024], P('dp', 'ctx')
- grad_first: float32 [1024, 2048], P('dp')
- grad_kernel: float32 [31, 1024], replicated
Inputs may be any that keep to these rules, and one draw needn't show every extreme that they name: Recording b has frames[b] real frames at the start and padding after them; some recording is full.
All inputs are finite; a program needn't handle non-finite values.
Results may differ from a plain program's by a relative error of at most 0.025.
Values may be sent and summed in bfloat16 or wider, within the bound.
No kernel may reach another device: no remote copies, remote signals or barrier semaphores. Data moves between devices by JAX's collectives and lax.ppermute only.
A program may use at most 128 MiB of HBM per device.

v0:
```python
import functools

import jax
import jax.numpy as jnp
from jax import lax
from jax.experimental import pallas as pl
from jax.experimental.pallas import tpu as pltpu
from jax.sharding import Mesh
from jax.sharding import PartitionSpec as P

HEADS = 16
EPSILON = 1e-05
BF = jnp.bfloat16
F32 = jnp.float32

DP = ("yh", "z", "core")
CTX = ("yl", "x")

VM = pl.BlockSpec(memory_space=pltpu.VMEM)
SM = pl.BlockSpec(memory_space=pltpu.SMEM)
ANY = pl.BlockSpec(memory_space=pl.ANY)


def params(mib, top=60):
    return pltpu.CompilerParams(vmem_limit_bytes=max(mib, top) << 20)


def cost(flops, nbytes):
    return pl.CostEstimate(flops=flops, bytes_accessed=nbytes, transcendentals=0)


def centred(values):
    centre = values - jnp.mean(values, -1, keepdims=True)
    spread = jnp.mean(centre * centre, -1, keepdims=True)
    return centre, lax.rsqrt(spread + EPSILON)


def norm_pull(cot, centre, inv):
    xhat = centre * inv
    return inv * (
        cot - jnp.mean(cot, -1, keepdims=True) - xhat * jnp.mean(cot * xhat, -1, keepdims=True)
    )


def dot(a, b):
    return jnp.dot(a, b, preferred_element_type=F32)


def dot_t(a, b):
    return lax.dot_general(a, b, (((1,), (1,)), ((), ())), preferred_element_type=F32)


def sigmoid(v):
    return jax.nn.sigmoid(v)


def whole(shape):
    return pl.BlockSpec(shape, lambda i: (0,) * len(shape))


def call(body, outs, ins, name, mib, scratch=(), anys=()):
    specs = [SM] + [whole(v.shape) for v in ins[1:]] + [ANY] * len(anys)
    return pl.pallas_call(
        body,
        grid=(1,),
        out_shape=tuple(jax.ShapeDtypeStruct(*o) for o in outs),
        in_specs=specs,
        out_specs=tuple(whole(o[0]) for o in outs),
        scratch_shapes=list(scratch),
        compiler_params=params(mib),
        name=name,
    )(*ins, *anys)


def ctx_index():
    return lax.axis_index("yl") * lax.axis_size("x") + lax.axis_index("x")


def at_lane(block, width):
    return pl.ds(pl.multiple_of(block * width, width), width)


def cut_body(blocks, scal, w2_ref, wq_ref, w1_ref, own_ref, w1_own_ref, next_ref):
    model = w2_ref.shape[1]
    width = model // blocks
    ctx = ctx_index()
    beside = lax.rem(ctx + blocks // 2, blocks)
    for ref, block in ((own_ref, ctx), (next_ref, beside)):
        ref[:, :model] = w2_ref[...]
        for part in range(3):
            lo = model + part * width
            ref[:, lo : lo + width] = wq_ref[:, at_lane(part * blocks + block, width)]
    for ref, lo, block in ((w1_own_ref, 0, ctx), (next_ref, model + 3 * width, beside)):
        for part in range(2):
            at = lo + part * width
            ref[:, at : at + width] = w1_ref[:, at_lane(part * blocks + block, width)]


def first_body(scal, x_ref, g_ref, out_ref):
    centre, inv = centred(x_ref[...].astype(F32))
    normed = (centre * inv * g_ref[...]).astype(BF)
    for i in range(out_ref.shape[0]):
        out_ref[i] = normed


def gate_body(taps, scal, x_ref, wm_ref, wo_ref, k_ref, conv_ref, hid_ref, gated_ref, w_s, pad_s):
    rec = pl.program_id(0)
    blocks, _, local, model = x_ref.shape
    length = blocks * local
    width = k_ref.shape[1]

    @pl.when(rec == 0)
    def _():
        core, yh, z = lax.axis_index("core"), lax.axis_index("yh"), lax.axis_index("z")
        zs = wm_ref.shape[0]
        for s in range(zs):
            owner = lax.rem(z - s + zs, zs)
            for slot, side in ((0, yh), (1, 1 - yh)):
                w_s[side, owner, core] = wm_ref[s, slot]
                w_s[side, owner, 1 - core] = wo_ref[s, slot]

    x = x_ref[...].reshape(length, model)
    hidden = dot(x, w_s[...].reshape(model, 2 * width))
    hid_ref[0] = hidden
    frames = scal[rec]
    here = lax.broadcasted_iota(jnp.int32, (length, width), 0) < frames
    gated = jnp.where(here, hidden[:, :width] * sigmoid(hidden[:, width:]), 0.0).astype(BF)
    gated_ref[0] = gated
    pad_s[0:16] = jnp.zeros((16, width), F32)
    pad_s[16 + length : 32 + length] = jnp.zeros((16, width), F32)
    pad_s[16 : 16 + length] = gated.astype(F32)
    for b in range(blocks):
        total = jnp.zeros((local, width), F32)
        for j in range(taps):
            at = b * local + j + 1
            total = total + k_ref[j : j + 1, :] * pad_s[at : at + local, :]
        conv_ref[b, 0] = total.astype(BF)


def fetch(pieces, slots, yh, core, sems):
    copies = []
    for dst, lo, width in slots:
        group = []
        for src, owner in pieces:
            for slot in range(2):
                side = yh if slot == 0 else 1 - yh
                group.append(
                    pltpu.make_async_copy(
                        src.at[:, slot, :, lo : lo + width],
                        dst.at[side, :, owner],
                        sems.at[len(copies) * 4 + len(group)],
                    )
                )
        copies.append(group)
    for group in copies:
        for one in group:
            one.start()
    return copies


def finish(group):
    for one in group:
        one.wait()


def token_body(
    blocks, scal, c_ref, x_ref, go_ref, g2_ref, ga_ref, mine, other, sent_ref, res_ref, gc_ref, w2_s, sems
):
    model = x_ref.shape[1]
    width = model // blocks
    copies = fetch(
        ((mine, lax.axis_index("core")), (other, 1 - lax.axis_index("core"))), ((w2_s, 0, model),), lax.axis_index("yh"), lax.axis_index("core"), sems
    )
    conv = jnp.concatenate([c_ref[i] for i in range(blocks)], 1).astype(F32)
    centre, inv = centred(conv)
    gain = g2_ref[...]
    normal = centre * inv * gain
    opening = sigmoid(normal)
    swished = (normal * opening).astype(BF)
    finish(copies[0])
    w2 = w2_s[...].reshape(model, model)
    back_two = dot_t(go_ref[...], w2)
    slope = opening + normal * opening * (1.0 - opening)
    grad_conv = norm_pull(back_two * slope * gain, centre, inv).astype(BF)
    for i in range(blocks):
        gc_ref[i] = grad_conv[:, i * width : (i + 1) * width]
    residual = (x_ref[...].astype(F32) + dot(swished, w2)).astype(BF)
    res_ref[...] = residual
    centre, inv = centred(residual.astype(F32))
    attn_in = (centre * inv * ga_ref[...]).astype(BF)
    for i in range(blocks):
        sent_ref[i] = attn_in


def back_body(
    taps, scal, gc_ref, hid_ref, gated_ref, x_ref, k_ref,
    gh_ref, keep_ref, send_ref, gk_ref, pad_s, gpad_s, gf_s, gk_s,
):
    rec = pl.program_id(0)
    core = lax.axis_index("core")
    frames = scal[rec]
    blocks, _, local, _ = gh_ref.shape
    length = blocks * local
    width = k_ref.shape[1]
    model = x_ref.shape[3]

    @pl.when(rec == 0)
    def _():
        gk_s[...] = jnp.zeros_like(gk_s)

    zeros = jnp.zeros((16, width), F32)
    for ref in (pad_s, gpad_s):
        ref[0:16] = zeros
        ref[16 + length : 32 + length] = zeros
    pad_s[16 : 16 + length] = gc_ref[...].reshape(length, width).astype(F32)
    gpad_s[16 : 16 + length] = gated_ref[0].astype(F32)
    for b in range(blocks):
        base = b * local
        total = jnp.zeros((local, width), F32)
        own = pad_s[16 + base : 16 + base + local, :]
        for j in range(taps):
            at = base + taps - j
            total = total + k_ref[j : j + 1, :] * pad_s[at : at + local, :]
            at = base + j + 1
            term = (gpad_s[at : at + local, :] * own).reshape(local // 8, 8, width)
            gk_s[j] += jnp.sum(term, 0)
        at = lax.broadcasted_iota(jnp.int32, (local, width), 0) + base
        grad_gated = jnp.where(at < frames, total, 0.0)
        linear = hid_ref[0, base : base + local, :width]
        opening = sigmoid(hid_ref[0, base : base + local, width:])
        first = grad_gated * opening
        gh_ref[b, 0, :, :width] = first.astype(BF)
        gh_ref[b, 0, :, width:] = (first * linear * (1.0 - opening)).astype(BF)
    grad_hidden = gh_ref[...].reshape(length, 2 * width)
    x = x_ref[...].reshape(length, model)
    grad_first = lax.dot_general(
        x, grad_hidden, (((0,), (0,)), ((), ())), preferred_element_type=F32
    ).reshape(gf_s.shape)

    @pl.when(rec == 0)
    def _():
        gf_s[...] = grad_first

    @pl.when(rec > 0)
    def _():
        gf_s[...] += grad_first

    @pl.when(rec == pl.num_programs(0) - 1)
    def _():
        keep_ref[...] = gf_s[:, :, pl.ds(core, 1)][:, :, 0]
        send_ref[...] = gf_s[:, :, pl.ds(1 - core, 1)][:, :, 0].astype(BF)
        gk = jnp.sum(gk_s[...], 1)
        half = gk_ref.shape[0]
        gk_ref[:, :width] = gk[:half]
        gk_ref[:, width:] = gk[half:]


def heads_body(head_dim, scal, x_ref, gh_ref, mine, other, out_ref, w_s, sems):
    rec = pl.program_id(0)
    frames = scal[rec]
    blocks, _, local, model = x_ref.shape
    length = blocks * local
    width = model // blocks

    @pl.when(rec == 0)
    def _():
        core = lax.axis_index("core")
        copies = fetch(
            ((mine, core), (other, 1 - core)), ((w_s, model, 3 * width),), lax.axis_index("yh"), core, sems
        )
        finish(copies[0])

    out_ref[:, :, :, : 2 * width] = gh_ref[...]
    x = x_ref[...].reshape(length, model)
    packed = dot(x, w_s[...].reshape(model, 3 * width)).astype(BF)
    q = packed[:, :width]
    k = packed[:, width : 2 * width]
    v = packed[:, 2 * width :]
    rows = min(256, length)
    key_ok = lax.broadcasted_iota(jnp.int32, (rows, length), 1) < frames
    lane = lax.broadcasted_iota(jnp.int32, (rows, width), 1)
    scaling = head_dim**-0.5
    for r in range(0, length, rows):
        qr = q[r : r + rows]
        attended = jnp.zeros((rows, width), F32)
        for h in range(width // head_dim):
            mine_h = (lane >= h * head_dim) & (lane < (h + 1) * head_dim)
            scores = dot_t(jnp.where(mine_h, qr, jnp.zeros_like(qr)), k) * scaling
            scores = jnp.where(key_ok, scores, -1e30)
            top = jnp.max(scores, -1, keepdims=True)
            numer = jnp.where(key_ok, jnp.exp(scores - top), 0.0)
            denom = jnp.sum(numer, -1, keepdims=True)
            attended = jnp.where(mine_h, dot(numer.astype(BF), v) / denom, attended)
        got = attended.astype(BF).reshape(rows // local, local, width)
        out_ref[r // local : (r + rows) // local, 0, :, 2 * width :] = got


def pair_body(scal, keep_ref, recv_ref, gk_ref, gkr_ref, *refs):
    zs = len(refs) - 1
    outs, both_s = refs[:zs], refs[zs]
    depth = keep_ref.shape[2]
    both_s[...] = (keep_ref[...] + recv_ref[...].astype(F32)).astype(BF)
    gk = (gk_ref[...] + gkr_ref[...]).astype(BF)
    for s in range(zs):
        to = lax.rem(lax.axis_index("z") + s, zs)
        for side in range(2):
            outs[s][side, :depth] = both_s[side, to]
            outs[s][side, depth:] = gk


def sum_body(scal, *refs):
    keep_ref, send_ref, total_s = refs[-3:]
    total = refs[0][...].astype(F32)
    for ref in refs[1:-3]:
        total = total + ref[...].astype(F32)
    total_s[...] = total
    keep_ref[...] = total_s[lax.axis_index("yh")].astype(BF)
    send_ref[...] = total_s[1 - lax.axis_index("yh")].astype(BF)


def last_body(scal, x_ref, gf_ref, gk_ref):
    blocks = x_ref.shape[0]
    depth, taps = gf_ref.shape[0], gk_ref.shape[0]
    model = gk_ref.shape[1]
    width = model // blocks
    half = x_ref.shape[2] - depth
    for i in range(blocks):
        lo = i * width
        total = x_ref[i, 0].astype(F32) + x_ref[(i + blocks // 2) % blocks, 1].astype(F32)
        gf_ref[:, lo : lo + width] = total[:depth, :width]
        gf_ref[:, model + lo : model + lo + width] = total[:depth, width:]
        gk_ref[:half, lo : lo + width] = total[depth:, :width]
        gk_ref[half:, lo : lo + width] = total[depth : depth + taps - half, width:]


def result_body(scal, a_ref, res_ref, x_ref, go_ref, g1_ref, mine, other, out_ref, gin_ref, wp_s, w1_s, sems):
    yh, core, ctx = lax.axis_index("yh"), lax.axis_index("core"), ctx_index()
    rows, model = x_ref.shape
    blocks = a_ref.shape[0]
    width = model // blocks
    copies = fetch(
        ((mine, core), (other, 1 - core)),
        ((wp_s, 0, model), (w1_s, model, 2 * model)),
        yh,
        core,
        sems,
    )
    centre, inv = centred(x_ref[...].astype(F32))
    attended = jnp.concatenate([a_ref[i, :, 2 * width :] for i in range(blocks)], 1)
    linear = jnp.concatenate([a_ref[i, :, :width] for i in range(blocks)], 1)
    gating = jnp.concatenate([a_ref[i, :, width : 2 * width] for i in range(blocks)], 1)
    finish(copies[0])
    projected = dot(attended, wp_s[...].reshape(model, model))
    records = 2
    local = rows // records
    at = lax.broadcasted_iota(jnp.int32, (local, model), 0) + ctx * local
    present = jnp.concatenate(
        [(at < scal[r]).astype(F32) for r in range(records)], 0
    )
    out_ref[...] = (res_ref[...].astype(F32) + present * projected).astype(BF)
    finish(copies[1])
    w1 = w1_s[...].reshape(model, 2 * model)
    back_one = dot_t(linear, w1[:, :model]) + dot_t(gating, w1[:, model:])
    pulled = norm_pull(back_one * g1_ref[...], centre, inv)
    gin_ref[...] = (go_ref[...].astype(F32) + pulled).astype(BF)


def swap_core(v):
    return lax.ppermute(v, "core", [(0, 1), (1, 0)])


def swap_yh(v):
    return lax.ppermute(v, ("yh", "yl"), [(0, 3), (3, 0), (1, 2), (2, 1)])


def shifted(v, axis, by):
    count = lax.axis_size(axis)
    return lax.ppermute(v, axis, [(i, (i + by) % count) for i in range(count)])


def local(
    inputs,
    frames,
    gain_first,
    w_first,
    depth_kernel,
    gain_second,
    w_second,
    gain_attn,
    w_qkv,
    w_proj,
    grad_out,
):
    records, local_len, model = inputs.shape
    taps = depth_kernel.shape[0]
    blocks = lax.axis_size(CTX)
    zs = lax.axis_size("z")
    depth = w_first.shape[0]
    width = model // blocks
    length = blocks * local_len
    rows = records * local_len
    head_dim = model // HEADS
    ctx = lax.axis_index(CTX)
    shape = jax.ShapeDtypeStruct
    barrier = lax.optimization_barrier

    scal = frames
    x = inputs.reshape(rows, model)
    cot = grad_out.reshape(rows, model)
    taps_own = lax.dynamic_slice_in_dim(
        jnp.pad(depth_kernel, ((0, 32 - taps), (0, 0))), ctx * width, width, 1
    )

    part = model + 3 * width
    own, w1_own, beside = call(
        functools.partial(cut_body, blocks),
        [((depth, part), BF), ((depth, 2 * width), BF), ((depth, part + 2 * width), BF)],
        [scal, w_second, w_qkv, w_first],
        "cut",
        16,
    )
    beside = swap_yh(beside)
    (sent,) = call(
        first_body, [((blocks, rows, model), BF)], [scal, x, gain_first.reshape(1, model)], "first_norm", 32
    )
    shard_a = jnp.stack([own, beside[:, :part]])
    w1_part = jnp.stack([w1_own, beside[:, part:]])
    shard_a, w1_part, sent = barrier((shard_a, w1_part, sent))
    all_a = lax.all_gather(shard_a, "z", axis=0, tiled=False)
    w1_mine = jnp.stack([w1_part] + [shifted(w1_part, "z", s) for s in range(1, zs)])
    w1_other = swap_core(w1_mine)
    normed = lax.all_to_all(sent, CTX, 0, 0, tiled=True).reshape(blocks, records, local_len, model)
    cat_b = jnp.concatenate([w_proj, w_first], 1)
    shard_b = jnp.stack([cat_b, swap_yh(cat_b)])

    by_record = lambda *rest: pl.BlockSpec(
        (blocks, 1, local_len) + rest, lambda r: (0, r, 0) + (0,) * len(rest)
    )
    of_record = lambda wide: pl.BlockSpec((1, length, wide), lambda r: (r, 0, 0))
    conv, hidden, gated = pl.pallas_call(
        functools.partial(gate_body, taps),
        grid=(records,),
        out_shape=(
            shape((blocks, records, local_len, width), BF),
            shape((records, length, 2 * width), F32),
            shape((records, length, width), BF),
        ),
        in_specs=[
            SM,
            by_record(model),
            whole((zs, 2, depth, 2 * width)),
            whole((zs, 2, depth, 2 * width)),
            whole((32, width)),
        ],
        out_specs=(by_record(width), of_record(2 * width), of_record(width)),
        scratch_shapes=[
            pltpu.VMEM((2, zs, 2, depth, 2 * width), BF),
            pltpu.VMEM((length + 32, width), F32),
        ],
        compiler_params=params(32),
        name="gate_conv",
    )(scal, normed, w1_mine, w1_other, taps_own)

    all_a, conv = barrier((all_a, conv))
    other_a = swap_core(all_a)
    shard_b, all_a = barrier((shard_b, all_a))
    all_b = lax.all_gather(shard_b, "z", axis=0, tiled=False)
    conv_rows = lax.all_to_all(conv, CTX, 0, 0, tiled=True).reshape(blocks, rows, width)

    sent, residual, grad_conv = call(
        functools.partial(token_body, blocks),
        [((blocks, rows, model), BF), ((rows, model), BF), ((blocks, rows, width), BF)],
        [scal, conv_rows, x, cot, gain_second.reshape(1, model), gain_attn.reshape(1, model)],
        "token_rows",
        32,
        [
            pltpu.VMEM((2, zs, 2, depth, model), BF),
            pltpu.SemaphoreType.DMA((4,)),
        ],
        [all_a, other_a],
    )
    grad_conv = lax.all_to_all(grad_conv, CTX, 0, 0, tiled=True)
    sent, grad_conv = barrier((sent, grad_conv))
    grad_conv = grad_conv.reshape(blocks, records, local_len, width)

    attn_in = lax.all_to_all(sent, CTX, 0, 0, tiled=True)
    attn_in = attn_in.reshape(blocks, records, local_len, model)
    share = (2, zs, depth, 2 * width)
    keep_spec = whole(share)

    grad_hidden, keep, send, gk = pl.pallas_call(
        functools.partial(back_body, taps),
        grid=(records,),
        out_shape=(
            shape((blocks, records, local_len, 2 * width), BF),
            shape(share, F32),
            shape(share, BF),
            shape((16, 2 * width), F32),
        ),
        in_specs=[
            SM, by_record(width), of_record(2 * width), of_record(width), by_record(model),
            whole((32, width)),
        ],
        out_specs=(by_record(2 * width), keep_spec, keep_spec, whole((16, 2 * width))),
        scratch_shapes=[
            pltpu.VMEM((length + 32, width), F32),
            pltpu.VMEM((length + 32, width), F32),
            pltpu.VMEM((2, zs, 2, depth, 2 * width), F32),
            pltpu.VMEM((32, 8, width), F32),
        ],
        compiler_params=params(32),
        name="conv_back",
    )(scal, grad_conv, hidden, gated, normed, taps_own)

    chunk = (2, depth + 16, 2 * width)
    chunks = call(
        pair_body,
        [(chunk, BF)] * zs,
        [scal, keep, swap_core(send), gk, swap_core(gk)],
        "pair_sum",
        16,
        [pltpu.VMEM(share, BF)],
    )
    sums = [chunks[0]] + [shifted(chunks[s], "z", s) for s in range(1, zs)]
    keep, send = call(
        sum_body, [(chunk[1:], BF)] * 2, [scal] + sums, "share_sum", 16, [pltpu.VMEM(chunk, F32)]
    )
    pair = jnp.stack([keep, swap_yh(send)])

    back = pl.pallas_call(
        functools.partial(heads_body, head_dim),
        grid=(records,),
        out_shape=shape((blocks, records, local_len, 3 * width), BF),
        in_specs=[SM, by_record(model), by_record(2 * width), ANY, ANY],
        out_specs=by_record(3 * width),
        scratch_shapes=[
            pltpu.VMEM((2, zs, 2, depth, 3 * width), BF),
            pltpu.SemaphoreType.DMA((4,)),
        ],
        compiler_params=params(32),
        name="heads",
    )(scal, attn_in, grad_hidden, all_a, other_a)

    all_b, back = barrier((all_b, back))
    other_b = swap_core(all_b)
    back = lax.all_to_all(back, CTX, 0, 0, tiled=True).reshape(blocks, rows, 3 * width)
    pair, back = barrier((pair, back))
    pair = lax.all_to_all(jnp.broadcast_to(pair, (blocks,) + chunk), CTX, 0, 0, tiled=True)
    grad_first, grad_kernel = call(
        last_body,
        [((depth, 2 * model), F32), ((taps, model), F32)],
        [scal, pair],
        "lay_out",
        16,
    )
    result, grad_in = call(
        result_body,
        [((rows, model), BF), ((rows, model), BF)],
        [scal, back, residual, x, cot, gain_first.reshape(1, model)],
        "result_rows",
        40,
        [
            pltpu.VMEM((2, zs, 2, depth, model), BF),
            pltpu.VMEM((2, zs, 2, depth, 2 * model), BF),
            pltpu.SemaphoreType.DMA((8,)),
        ],
        [all_b, other_b],
    )
    return (
        result.reshape(records, local_len, model),
        grad_in.reshape(records, local_len, model),
        grad_first,
        grad_kernel,
    )


def solution(mesh):
    dp, ctx = mesh.devices.shape
    split = Mesh(
        mesh.devices.reshape(2, dp // 4, 2, 2, ctx // 2), ("yh", "z", "core", "yl", "x")
    )
    tokens = P(DP, CTX, None)
    placed = (
        tokens,
        P(DP),
        P(),
        P(DP, None),
        P(),
        P(),
        P(DP, None),
        P(),
        P(DP, None),
        P(DP, None),
        tokens,
    )
    return jax.shard_map(
        local,
        mesh=split,
        in_specs=placed,
        out_specs=(tokens, tokens, P(DP, None), P()),
        check_vma=False,
    )
```

profile of v0, /device:TPU:8, one launch (start us, length us, event | category | flops | bytes accessed | tf_op | source)
XLA Modules:
  0.0 199.2 jit_solution(17865443299967266464)
XLA Ops:
  10.7 2.6 %first_norm.1 = bf16[8,128,1024]{2,1,0:T(8,128)(2,1)} custom-call(s32[2]{0:T(128)} %scal.19, bf16[128,1024]{1,0:T(8,128)(2,1)} %bitcast.48, f32[1,1024]{1,0:T(1,128)} %bitcast.60), custom_call_target="tpu_custom_call" | custom-call | tf_op jit(solution)/shard_map/first_norm/pallas_call | solution.py:63
  19.0 3.3 %collective-permute-start.2 = (bf16[2,32,256]{2,1,0:T(8,128)(2,1)S(1)}, bf16[2,32,256]{2,1,0:T(8,128)(2,1)S(1)}, u32[]{:S(2)}, u32[]{:S(2)}) collective-permute-start(bf16[2,32,256]{2,1,0:T(8,128)(2,1)S(1)} %pad_maximum_fusion.3), channel_id=1, source_target_pairs={{0,32},{16,48},{32,64},{48,80},{64,96},{80,112},{96,0},{112,16},{1... | collective-permute-start | bytes 98312 | tf_op jit(solution)/shard_map/ppermute | solution.py:378
  22.3 4.0 %collective-permute-start.3 = (bf16[2,32,256]{2,1,0:T(8,128)(2,1)S(1)}, bf16[2,32,256]{2,1,0:T(8,128)(2,1)S(1)}, u32[]{:S(2)}, u32[]{:S(2)}) collective-permute-start(bf16[2,32,256]{2,1,0:T(8,128)(2,1)S(1)} %pad_maximum_fusion.3), channel_id=1, source_target_pairs={{0,48},{16,64},{32,80},{48,96},{64,112},{80,0},{96,16},{112,32},{1... | collective-permute-start | bytes 98312 | tf_op jit(solution)/shard_map/ppermute | solution.py:378
  26.9 7.4 %all-to-all-start = ((bf16[8,128,1024]{2,1,0:T(8,128)(2,1)}), bf16[8,128,1024]{2,1,0:T(8,128)(2,1)S(1)}, u32[]{:S(2)}, u32[]{:S(2)}) async-start(bf16[8,128,1024]{2,1,0:T(8,128)(2,1)} %first_norm.1), calls=%async_computation | async-start | bytes 4194304 | tf_op jit(solution)/shard_map/all_to_all | solution.py:432
  34.3 5.0 %collective-permute-start.5 = (bf16[2,32,256]{2,1,0:T(8,128)(2,1)S(1)}, bf16[2,32,256]{2,1,0:T(8,128)(2,1)S(1)}, u32[]{:S(2)}, u32[]{:S(2)}) collective-permute-start(bf16[2,32,256]{2,1,0:T(8,128)(2,1)S(1)} %pad_maximum_fusion.3), channel_id=1, source_target_pairs={{0,80},{16,96},{32,112},{48,0},{64,16},{80,32},{96,48},{112,64},{1... | collective-permute-start | bytes 98312 | tf_op jit(solution)/shard_map/ppermute | solution.py:378
  39.3 2.7 %collective-permute-start.6 = (bf16[2,32,256]{2,1,0:T(8,128)(2,1)S(1)}, bf16[2,32,256]{2,1,0:T(8,128)(2,1)S(1)}, u32[]{:S(2)}, u32[]{:S(2)}) collective-permute-start(bf16[2,32,256]{2,1,0:T(8,128)(2,1)S(1)} %pad_maximum_fusion.3), channel_id=1, source_target_pairs={{0,96},{16,112},{32,0},{48,16},{64,32},{80,48},{96,64},{112,80},{1... | collective-permute-start | bytes 98312 | tf_op jit(solution)/shard_map/ppermute | solution.py:378
  47.7 9.7 %all-to-all-done = bf16[8,128,1024]{2,1,0:T(8,128)(2,1)S(1)} async-done(((bf16[8,128,1024]{2,1,0:T(8,128)(2,1)}), bf16[8,128,1024]{2,1,0:T(8,128)(2,1)S(1)}, u32[]{:S(2)}, u32[]{:S(2)}) %all-to-all-start) | async-done | bytes 2097184 | tf_op jit(solution)/shard_map/all_to_all | solution.py:432
  58.7 4.4 %gate_conv.1 = (bf16[8,2,64,128]{3,2,1,0:T(8,128)(2,1)}, f32[2,512,256]{2,1,0:T(8,128)}, bf16[2,512,128]{2,1,0:T(8,128)(2,1)}) custom-call(s32[2]{0:T(128)} %scal.19, bf16[8,2,64,1024]{3,2,1,0:T(8,128)(2,1)} %bitcast.40, bf16[8,2,32,256]{3,2,1,0:T(8,128)(2,1)} %copy-done.5, bf16[8,2,32,256]{3,2,1,0:T(8,128)(2,1)} %copy-done.6, ...), custom_call_target="tpu_custom_call" | custom-call | tf_op jit(solution)/shard_map/gate_conv/pallas_call | solution.py:440
  63.2 12.2 %all_to_all.30 = bf16[8,2,64,128]{3,2,1,0:T(8,128)(2,1)} all-to-all(bf16[8,2,64,128]{3,2,1,0:T(8,128)(2,1)} %get-tuple-element.51), channel_id=1, replica_groups=mesh['yh'=2,'z'=8,'core'=2,'yl'=2,'x'=4] {'yl','x'}, dimensions={0} | all-to-all | bytes 524288 | tf_op jit(solution)/shard_map/all_to_all | solution.py:468
  76.5 5.6 %token_rows.1 = (bf16[8,128,1024]{2,1,0:T(8,128)(2,1)}, bf16[128,1024]{1,0:T(8,128)(2,1)}, bf16[8,128,128]{2,1,0:T(8,128)(2,1)}) custom-call(s32[2]{0:T(128)} %scal.19, bf16[8,128,128]{2,1,0:T(8,128)(2,1)} %bitcast.54, bf16[128,1024]{1,0:T(8,128)(2,1)} %bitcast.49, bf16[128,1024]{1,0:T(8,128)(2,1)} %bitcast.51, f32[1,1024]{1,0:T(1,128)} %bitcast.63, ...), custom_call_target="tpu_custom_call" | custom-call | tf_op jit(solution)/shard_map/token_rows/pallas_call | solution.py:63
  82.2 11.6 %all_to_all.31 = bf16[8,128,128]{2,1,0:T(8,128)(2,1)} all-to-all(bf16[8,128,128]{2,1,0:T(8,128)(2,1)} %get-tuple-element.55), channel_id=1, replica_groups=mesh['yh'=2,'z'=8,'core'=2,'yl'=2,'x'=4] {'yl','x'}, dimensions={0} | all-to-all | bytes 524288 | tf_op jit(solution)/shard_map/all_to_all | solution.py:482
  93.7 5.0 %all-to-all-start.3 = ((bf16[8,128,1024]{2,1,0:T(8,128)(2,1)}), bf16[8,128,1024]{2,1,0:T(8,128)(2,1)S(1)}, u32[]{:S(2)}, u32[]{:S(2)}) async-start(bf16[8,128,1024]{2,1,0:T(8,128)(2,1)} %get-tuple-element.73), calls=%async_computation.3 | async-start | bytes 4194304 | tf_op jit(solution)/shard_map/all_to_all | solution.py:486
  98.7 6.2 %conv_back.1 = (bf16[8,2,64,256]{3,2,1,0:T(8,128)(2,1)}, f32[2,8,32,256]{3,2,1,0:T(8,128)}, bf16[2,8,32,256]{3,2,1,0:T(8,128)(2,1)}, f32[16,256]{1,0:T(8,128)}) custom-call(s32[2]{0:T(128)} %scal.19, bf16[8,2,64,128]{3,2,1,0:T(8,128)(2,1)} %bitcast.53, f32[2,512,256]{2,1,0:T(8,128)} %get-tuple-element.57.hid_ref, ...), custom_call_target="tpu_custom_call" | custom-call | tf_op jit(solution)/shard_map/conv_back/pallas_call | solution.py:491
  105.0 18.5 %all-to-all-done.3 = bf16[8,128,1024]{2,1,0:T(8,128)(2,1)S(1)} async-done(((bf16[8,128,1024]{2,1,0:T(8,128)(2,1)}), bf16[8,128,1024]{2,1,0:T(8,128)(2,1)S(1)}, u32[]{:S(2)}, u32[]{:S(2)}) %all-to-all-start.3) | async-done | bytes 2097184 | tf_op jit(solution)/shard_map/all_to_all | solution.py:486
  124.8 7.5 %heads.1 = bf16[8,2,64,384]{3,2,1,0:T(8,128)(2,1)} custom-call(s32[2]{0:T(128)} %scal.19, bf16[8,2,64,1024]{3,2,1,0:T(8,128)(2,1)} %bitcast.42, bf16[8,2,64,256]{3,2,1,0:T(8,128)(2,1)} %get-tuple-element.74.gh_ref, bf16[8,2,32,1408]{3,2,1,0:T(8,128)(2,1)} %bitcast.45, bf16[8,2,32,1408]{3,2,1,0:T(8,128)(2,1)} %copy-done.2), custom_call_target="tpu_custom_call" | custom-call | tf_op jit(solution)/shard_map/heads/pallas_call | solution.py:530
  132.5 5.6 %all-to-all-start.4 = ((bf16[8,2,64,384]{3,2,1,0:T(8,128)(2,1)}), bf16[8,2,64,384]{3,2,1,0:T(8,128)(2,1)}, u32[]{:S(2)}, u32[]{:S(2)}) async-start(bf16[8,2,64,384]{3,2,1,0:T(8,128)(2,1)} %heads.1), calls=%async_computation.4 | async-start | bytes 1572864 | tf_op jit(solution)/shard_map/all_to_all | solution.py:546
  140.3 1.9 pair_sum.1
  144.0 3.5 %collective-permute-start.14 = (bf16[2,48,256]{2,1,0:T(8,128)(2,1)}, bf16[2,48,256]{2,1,0:T(8,128)(2,1)S(1)}, u32[]{:S(2)}, u32[]{:S(2)}) collective-permute-start(bf16[2,48,256]{2,1,0:T(8,128)(2,1)} %get-tuple-element.64), channel_id=1, source_target_pairs={{0,32},{16,48},{32,64},{48,80},{64,96},{80,112},{96,0},{112,16},{1... | collective-permute-start | bytes 147464 | tf_op jit(solution)/shard_map/ppermute | solution.py:378
  148.7 4.4 %collective-permute-start.16 = (bf16[2,48,256]{2,1,0:T(8,128)(2,1)}, bf16[2,48,256]{2,1,0:T(8,128)(2,1)S(1)}, u32[]{:S(2)}, u32[]{:S(2)}) collective-permute-start(bf16[2,48,256]{2,1,0:T(8,128)(2,1)} %get-tuple-element.66), channel_id=1, source_target_pairs={{0,64},{16,80},{32,96},{48,112},{64,0},{80,16},{96,32},{112,48},{1... | collective-permute-start | bytes 147464 | tf_op jit(solution)/shard_map/ppermute | solution.py:378
  153.8 3.8 %collective-permute-start.18 = (bf16[2,48,256]{2,1,0:T(8,128)(2,1)}, bf16[2,48,256]{2,1,0:T(8,128)(2,1)S(1)}, u32[]{:S(2)}, u32[]{:S(2)}) collective-permute-start(bf16[2,48,256]{2,1,0:T(8,128)(2,1)} %get-tuple-element.68), channel_id=1, source_target_pairs={{0,96},{16,112},{32,0},{48,16},{64,32},{80,48},{96,64},{112,80},{1... | collective-permute-start | bytes 147464 | tf_op jit(solution)/shard_map/ppermute | solution.py:378
  158.7 3.3 %collective-permute-done.17.refs_5_ = bf16[2,48,256]{2,1,0:T(8,128)(2,1)S(1)} collective-permute-done((bf16[2,48,256]{2,1,0:T(8,128)(2,1)}, bf16[2,48,256]{2,1,0:T(8,128)(2,1)S(1)}, u32[]{:S(2)}, u32[]{:S(2)}) %collective-permute-start.17) | collective-permute-done | bytes 49184 | tf_op jit(solution)/shard_map/ppermute | solution.py:378
  165.0 4.0 %collective-permute-done.20 = bf16[48,256]{1,0:T(8,128)(2,1)S(1)} collective-permute-done((bf16[48,256]{1,0:T(8,128)(2,1)}, bf16[48,256]{1,0:T(8,128)(2,1)S(1)}, u32[]{:S(2)}, u32[]{:S(2)}) %collective-permute-start.20) | collective-permute-done | bytes 24608 | tf_op jit(solution)/shard_map/ppermute | solution.py:373
  169.8 12.4 %all_to_all.32.x_ref = bf16[8,2,48,256]{3,2,1,0:T(8,128)(2,1)} all-to-all(bf16[8,2,48,256]{3,2,1,0:T(8,128)(2,1)S(1)} %broadcast_in_dim.3), channel_id=1, replica_groups=mesh['yh'=2,'z'=8,'core'=2,'yl'=2,'x'=4] {'yl','x'}, dimensions={0} | all-to-all | bytes 786432 | tf_op jit(solution)/shard_map/all_to_all | solution.py:548
  185.7 6.6 %result_rows.1 = (bf16[128,1024]{1,0:T(8,128)(2,1)}, bf16[128,1024]{1,0:T(8,128)(2,1)}) custom-call(s32[2]{0:T(128)} %scal.19, bf16[8,128,384]{2,1,0:T(8,128)(2,1)} %bitcast.27.a_ref, bf16[128,1024]{1,0:T(8,128)(2,1)} %get-tuple-element.77.res_ref, bf16[128,1024]{1,0:T(8,128)(2,1)} %bitcast.50, bf16[128,1024]{1,0:T(8,128)(2,1)} %bitcast.52, ...), custom_call_target="tpu_custom_call" | custom-call | tf_op jit(solution)/shard_map/result_rows/pallas_call | solution.py:63
  (107 shorter events, 33.5 us)
Async XLA Ops:
  7.2 55.9 %all-gather.5.cloned.1.call-start = ((), (), s32[]{:S(2)}) async-start(), calls=%async_computation.6 | async-start | bytes 1622016 | tf_op jit(solution)/shard_map/all_gather | solution.py:429
  9.1 4.9 %collective-permute-start = (bf16[32,1664]{1,0:T(8,128)(2,1)}, bf16[32,1664]{1,0:T(8,128)(2,1)S(1)}, u32[]{:S(2)}, u32[]{:S(2)}) collective-permute-start(bf16[32,1664]{1,0:T(8,128)(2,1)} %get-tuple-element.45), channel_id=1, source_target_pairs={{0,132},{132,0},{4,128},{128,4},{1,133},{133,1},{5,129},{129,5},{2... | collective-permute-start | bytes 319496 | tf_op jit(solution)/shard_map/ppermute | solution.py:373
  14.8 31.4 %collective-permute-start.9 = (bf16[32,3072]{1,0:T(8,128)(2,1)S(1)}, bf16[32,3072]{1,0:T(8,128)(2,1)S(1)}, u32[]{:S(2)}, u32[]{:S(2)}) collective-permute-start(bf16[32,3072]{1,0:T(8,128)(2,1)S(1)} %constant_dynamic-update-slice_fusion), channel_id=1, source_target_pairs={{0,132},{132,0},{4,128},{128,4},{1,133},{133,1},{5,129},{129,5},{2... | collective-permute-start | bytes 589832 | tf_op jit(solution)/shard_map/ppermute | solution.py:373
  17.1 17.2 %collective-permute-start.1 = (bf16[2,32,256]{2,1,0:T(8,128)(2,1)S(1)}, bf16[2,32,256]{2,1,0:T(8,128)(2,1)S(1)}, u32[]{:S(2)}, u32[]{:S(2)}) collective-permute-start(bf16[2,32,256]{2,1,0:T(8,128)(2,1)S(1)} %pad_maximum_fusion.3), channel_id=1, source_target_pairs={{0,16},{16,32},{32,48},{48,64},{64,80},{80,96},{96,112},{112,0},{1... | collective-permute-start | bytes 98312 | tf_op jit(solution)/shard_map/ppermute | solution.py:378
  19.0 20.3 %collective-permute-start.2 = (bf16[2,32,256]{2,1,0:T(8,128)(2,1)S(1)}, bf16[2,32,256]{2,1,0:T(8,128)(2,1)S(1)}, u32[]{:S(2)}, u32[]{:S(2)}) collective-permute-start(bf16[2,32,256]{2,1,0:T(8,128)(2,1)S(1)} %pad_maximum_fusion.3), channel_id=1, source_target_pairs={{0,32},{16,48},{32,64},{48,80},{64,96},{80,112},{96,0},{112,16},{1... | collective-permute-start | bytes 98312 | tf_op jit(solution)/shard_map/ppermute | solution.py:378
  22.3 19.7 %collective-permute-start.3 = (bf16[2,32,256]{2,1,0:T(8,128)(2,1)S(1)}, bf16[2,32,256]{2,1,0:T(8,128)(2,1)S(1)}, u32[]{:S(2)}, u32[]{:S(2)}) collective-permute-start(bf16[2,32,256]{2,1,0:T(8,128)(2,1)S(1)} %pad_maximum_fusion.3), channel_id=1, source_target_pairs={{0,48},{16,64},{32,80},{48,96},{64,112},{80,0},{96,16},{112,32},{1... | collective-permute-start | bytes 98312 | tf_op jit(solution)/shard_map/ppermute | solution.py:378
  26.3 16.7 %collective-permute-start.4 = (bf16[2,32,256]{2,1,0:T(8,128)(2,1)S(1)}, bf16[2,32,256]{2,1,0:T(8,128)(2,1)S(1)}, u32[]{:S(2)}, u32[]{:S(2)}) collective-permute-start(bf16[2,32,256]{2,1,0:T(8,128)(2,1)S(1)} %pad_maximum_fusion.3), channel_id=1, source_target_pairs={{0,64},{16,80},{32,96},{48,112},{64,0},{80,16},{96,32},{112,48},{1... | collective-permute-start | bytes 98312 | tf_op jit(solution)/shard_map/ppermute | solution.py:378
  26.9 30.5 %all-to-all-start = ((bf16[8,128,1024]{2,1,0:T(8,128)(2,1)}), bf16[8,128,1024]{2,1,0:T(8,128)(2,1)S(1)}, u32[]{:S(2)}, u32[]{:S(2)}) async-start(bf16[8,128,1024]{2,1,0:T(8,128)(2,1)} %first_norm.1), calls=%async_computation | async-start | bytes 4194304 | tf_op jit(solution)/shard_map/all_to_all | solution.py:432
  34.3 98.1 %all-gather.7.cloned.1.call-start = ((), (), s32[]{:S(2)}) async-start(), calls=%async_computation.7 | async-start | bytes 3538944 | tf_op jit(solution)/shard_map/all_gather | solution.py:467
  34.3 8.7 %collective-permute-start.5 = (bf16[2,32,256]{2,1,0:T(8,128)(2,1)S(1)}, bf16[2,32,256]{2,1,0:T(8,128)(2,1)S(1)}, u32[]{:S(2)}, u32[]{:S(2)}) collective-permute-start(bf16[2,32,256]{2,1,0:T(8,128)(2,1)S(1)} %pad_maximum_fusion.3), channel_id=1, source_target_pairs={{0,80},{16,96},{32,112},{48,0},{64,16},{80,32},{96,48},{112,64},{1... | collective-permute-start | bytes 98312 | tf_op jit(solution)/shard_map/ppermute | solution.py:378
  39.3 5.2 %collective-permute-start.6 = (bf16[2,32,256]{2,1,0:T(8,128)(2,1)S(1)}, bf16[2,32,256]{2,1,0:T(8,128)(2,1)S(1)}, u32[]{:S(2)}, u32[]{:S(2)}) collective-permute-start(bf16[2,32,256]{2,1,0:T(8,128)(2,1)S(1)} %pad_maximum_fusion.3), channel_id=1, source_target_pairs={{0,96},{16,112},{32,0},{48,16},{64,32},{80,48},{96,64},{112,80},{1... | collective-permute-start | bytes 98312 | tf_op jit(solution)/shard_map/ppermute | solution.py:378
  42.0 4.2 %collective-permute-start.7 = (bf16[2,32,256]{2,1,0:T(8,128)(2,1)S(1)}, bf16[2,32,256]{2,1,0:T(8,128)(2,1)S(1)}, u32[]{:S(2)}, u32[]{:S(2)}) collective-permute-start(bf16[2,32,256]{2,1,0:T(8,128)(2,1)S(1)} %pad_maximum_fusion.3), channel_id=1, source_target_pairs={{0,112},{16,0},{32,16},{48,32},{64,48},{80,64},{96,80},{112,96},{1... | collective-permute-start | bytes 98312 | tf_op jit(solution)/shard_map/ppermute | solution.py:378
  63.1 12.3 %collective-permute-start.10 = (bf16[8,2,32,1408]{3,2,1,0:T(8,128)(2,1)}, bf16[8,2,32,1408]{3,2,1,0:T(8,128)(2,1)S(1)}, u32[]{:S(2)}, u32[]{:S(2)}) collective-permute-start(bf16[8,2,32,1408]{3,2,1,0:T(8,128)(2,1)} %bitcast.43), channel_id=1, source_target_pairs={{0,8},{8,0},{1,9},{9,1},{2,10},{10,2},{3,11},{11,3},{4,12},{12,4},... | collective-permute-start | bytes 4325384 | tf_op jit(solution)/shard_map/ppermute | solution.py:369
  93.7 29.8 %all-to-all-start.3 = ((bf16[8,128,1024]{2,1,0:T(8,128)(2,1)}), bf16[8,128,1024]{2,1,0:T(8,128)(2,1)S(1)}, u32[]{:S(2)}, u32[]{:S(2)}) async-start(bf16[8,128,1024]{2,1,0:T(8,128)(2,1)} %get-tuple-element.73), calls=%async_computation.3 | async-start | bytes 4194304 | tf_op jit(solution)/shard_map/all_to_all | solution.py:486
  132.4 51.6 %collective-permute-start.21 = (bf16[8,2,32,3072]{3,2,1,0:T(8,128)(2,1)}, bf16[8,2,32,3072]{3,2,1,0:T(8,128)(2,1)S(1)}, u32[]{:S(2)}, u32[]{:S(2)}) collective-permute-start(bf16[8,2,32,3072]{3,2,1,0:T(8,128)(2,1)} %bitcast.46), channel_id=1, source_target_pairs={{0,8},{8,0},{1,9},{9,1},{2,10},{10,2},{3,11},{11,3},{4,12},{12,4},... | collective-permute-start | bytes 9437192 | tf_op jit(solution)/shard_map/ppermute | solution.py:369
  132.5 37.3 %all-to-all-start.4 = ((bf16[8,2,64,384]{3,2,1,0:T(8,128)(2,1)}), bf16[8,2,64,384]{3,2,1,0:T(8,128)(2,1)}, u32[]{:S(2)}, u32[]{:S(2)}) async-start(bf16[8,2,64,384]{3,2,1,0:T(8,128)(2,1)} %heads.1), calls=%async_computation.4 | async-start | bytes 1572864 | tf_op jit(solution)/shard_map/all_to_all | solution.py:546
  142.3 10.9 %collective-permute-start.13 = (bf16[2,48,256]{2,1,0:T(8,128)(2,1)}, bf16[2,48,256]{2,1,0:T(8,128)(2,1)S(1)}, u32[]{:S(2)}, u32[]{:S(2)}) collective-permute-start(bf16[2,48,256]{2,1,0:T(8,128)(2,1)} %get-tuple-element.63), channel_id=1, source_target_pairs={{0,16},{16,32},{32,48},{48,64},{64,80},{80,96},{96,112},{112,0},{1... | collective-permute-start | bytes 147464 | tf_op jit(solution)/shard_map/ppermute | solution.py:378
  144.0 9.8 %collective-permute-start.14 = (bf16[2,48,256]{2,1,0:T(8,128)(2,1)}, bf16[2,48,256]{2,1,0:T(8,128)(2,1)S(1)}, u32[]{:S(2)}, u32[]{:S(2)}) collective-permute-start(bf16[2,48,256]{2,1,0:T(8,128)(2,1)} %get-tuple-element.64), channel_id=1, source_target_pairs={{0,32},{16,48},{32,64},{48,80},{64,96},{80,112},{96,0},{112,16},{1... | collective-permute-start | bytes 147464 | tf_op jit(solution)/shard_map/ppermute | solution.py:378
  147.5 10.1 %collective-permute-start.15 = (bf16[2,48,256]{2,1,0:T(8,128)(2,1)}, bf16[2,48,256]{2,1,0:T(8,128)(2,1)S(1)}, u32[]{:S(2)}, u32[]{:S(2)}) collective-permute-start(bf16[2,48,256]{2,1,0:T(8,128)(2,1)} %get-tuple-element.65), channel_id=1, source_target_pairs={{0,48},{16,64},{32,80},{48,96},{64,112},{80,0},{96,16},{112,32},{1... | collective-permute-start | bytes 147464 | tf_op jit(solution)/shard_map/ppermute | solution.py:378
  148.7 9.9 %collective-permute-start.16 = (bf16[2,48,256]{2,1,0:T(8,128)(2,1)}, bf16[2,48,256]{2,1,0:T(8,128)(2,1)S(1)}, u32[]{:S(2)}, u32[]{:S(2)}) collective-permute-start(bf16[2,48,256]{2,1,0:T(8,128)(2,1)} %get-tuple-element.66), channel_id=1, source_target_pairs={{0,64},{16,80},{32,96},{48,112},{64,0},{80,16},{96,32},{112,48},{1... | collective-permute-start | bytes 147464 | tf_op jit(solution)/shard_map/ppermute | solution.py:378
  153.2 8.8 %collective-permute-start.17 = (bf16[2,48,256]{2,1,0:T(8,128)(2,1)}, bf16[2,48,256]{2,1,0:T(8,128)(2,1)S(1)}, u32[]{:S(2)}, u32[]{:S(2)}) collective-permute-start(bf16[2,48,256]{2,1,0:T(8,128)(2,1)} %get-tuple-element.67), channel_id=1, source_target_pairs={{0,80},{16,96},{32,112},{48,0},{64,16},{80,32},{96,48},{112,64},{1... | collective-permute-start | bytes 147464 | tf_op jit(solution)/shard_map/ppermute | solution.py:378
  153.8 8.3 %collective-permute-start.18 = (bf16[2,48,256]{2,1,0:T(8,128)(2,1)}, bf16[2,48,256]{2,1,0:T(8,128)(2,1)S(1)}, u32[]{:S(2)}, u32[]{:S(2)}) collective-permute-start(bf16[2,48,256]{2,1,0:T(8,128)(2,1)} %get-tuple-element.68), channel_id=1, source_target_pairs={{0,96},{16,112},{32,0},{48,16},{64,32},{80,48},{96,64},{112,80},{1... | collective-permute-start | bytes 147464 | tf_op jit(solution)/shard_map/ppermute | solution.py:378
  157.6 5.1 %collective-permute-start.19 = (bf16[2,48,256]{2,1,0:T(8,128)(2,1)}, bf16[2,48,256]{2,1,0:T(8,128)(2,1)S(1)}, u32[]{:S(2)}, u32[]{:S(2)}) collective-permute-start(bf16[2,48,256]{2,1,0:T(8,128)(2,1)} %get-tuple-element.69), channel_id=1, source_target_pairs={{0,112},{16,0},{32,16},{48,32},{64,48},{80,64},{96,80},{112,96},{1... | collective-permute-start | bytes 147464 | tf_op jit(solution)/shard_map/ppermute | solution.py:378
  165.0 4.0 %collective-permute-start.20 = (bf16[48,256]{1,0:T(8,128)(2,1)}, bf16[48,256]{1,0:T(8,128)(2,1)S(1)}, u32[]{:S(2)}, u32[]{:S(2)}) collective-permute-start(bf16[48,256]{1,0:T(8,128)(2,1)} %get-tuple-element.71), channel_id=1, source_target_pairs={{0,132},{132,0},{4,128},{128,4},{1,133},{133,1},{5,129},{129,5},{2... | collective-permute-start | bytes 73736 | tf_op jit(solution)/shard_map/ppermute | solution.py:373
  (25 other events, 123.5 us)
Sparse Core Ops, SparseCore 0:
  14.9 44.9 all-gather.4
  63.2 43.0 all-gather.6
where the time goes:
time: 200 us; the launch traced here: 199 us
  starting transfers between devices  56.8 us (28%)
  waiting for transfers between devices  41.9 us (21%)
  Pallas kernels  40.2 us (20%)
  blocking collectives  36.2 us (18%)
  between operations  14.3 us (7%)
  local copies, waits for them, and re-layouts  7.45 us (4%)
  other arithmetic  2.28 us (1%)
    ppermute x14, starting transfers between devices, shifted(): return lax.ppermute(v, axis, [(i, (i + by) % count) for i in range(count)])  34.9 us
    pallas_call x7, Pallas kernels, call(): pl.pallas_call(body, grid=(1,), out_shape=tuple((jax.ShapeDtypeStruct(*o)...  22.1 us
    all_to_all x1, waiting for transfers between devices, local(): attn_in = lax.all_to_all(sent, CTX, 0, 0, tiled=True)  18.5 us
    all_to_all x1, blocking collectives, local(): lax.all_to_all(jnp.broadcast_to(pair, (blocks,) + chunk), CTX, 0, 0, tile...  12.4 us
    all_to_all x1, blocking collectives, local(): lax.all_to_all(conv, CTX, 0, 0, tiled=True).reshape(blocks, rows, width)  12.2 us
    all_to_all x1, blocking collectives, local(): grad_conv = lax.all_to_all(grad_conv, CTX, 0, 0, tiled=True)  11.6 us
    all_to_all x1, waiting for transfers between devices, local(): lax.all_to_all(sent, CTX, 0, 0, tiled=True)  9.65 us
    pallas_call x1, Pallas kernels, local(): pl.pallas_call(functools.partial(heads_body, head_dim), grid=(records,),...  7.53 us
  transfers between devices with their start and end apart: 27, of which 11 were waited for; matrix products, arithmetic and copies ran while one was open for 1% of the time, Pallas kernels for 16%

commit v1 on v0

--- a/solution.py
+++ b/solution.py
@@ -58,7 +58,7 @@
     return pl.BlockSpec(shape, lambda i: (0,) * len(shape))
 
 
-def call(body, outs, ins, name, mib, scratch=(), anys=()):
+def call(body, outs, ins, name, mib, scratch=(), anys=(), hint=0):
     specs = [SM] + [whole(v.shape) for v in ins[1:]] + [ANY] * len(anys)
     return pl.pallas_call(
         body,
@@ -68,6 +68,7 @@
         out_specs=tuple(whole(o[0]) for o in outs),
         scratch_shapes=list(scratch),
         compiler_params=params(mib),
+        cost_estimate=cost(hint, hint // 300) if hint else None,
         name=name,
     )(*ins, *anys)
 
@@ -96,6 +97,11 @@
             ref[:, at : at + width] = w1_ref[:, at_lane(part * blocks + block, width)]
 
 
+def beside_body(lo, scal, own_ref, next_ref, out_ref):
+    out_ref[0] = own_ref[...]
+    out_ref[1] = next_ref[:, lo : lo + own_ref.shape[1]]
+
+
 def first_body(scal, x_ref, g_ref, out_ref):
     centre, inv = centred(x_ref[...].astype(F32))
     normed = (centre * inv * g_ref[...]).astype(BF)
@@ -114,7 +120,7 @@
         core, yh, z = lax.axis_index("core"), lax.axis_index("yh"), lax.axis_index("z")
         zs = wm_ref.shape[0]
         for s in range(zs):
-            owner = lax.rem(z - s + zs, zs)
+            owner = z ^ s
             for slot, side in ((0, yh), (1, 1 - yh)):
                 w_s[side, owner, core] = wm_ref[s, slot]
                 w_s[side, owner, 1 - core] = wo_ref[s, slot]
@@ -423,11 +429,23 @@
     (sent,) = call(
         first_body, [((blocks, rows, model), BF)], [scal, x, gain_first.reshape(1, model)], "first_norm", 32
     )
-    shard_a = jnp.stack([own, beside[:, :part]])
-    w1_part = jnp.stack([w1_own, beside[:, part:]])
-    shard_a, w1_part, sent = barrier((shard_a, w1_part, sent))
+    (shard_a,) = call(
+        functools.partial(beside_body, 0), [((2,) + own.shape, BF)], [scal, own, beside], "beside_a", 16
+    )
+    (w1_part,) = call(
+        functools.partial(beside_body, part),
+        [((2,) + w1_own.shape, BF)],
+        [scal, w1_own, beside],
+        "beside_w1",
+        16,
+        hint=int(3e10),
+    )
     all_a = lax.all_gather(shard_a, "z", axis=0, tiled=False)
-    w1_mine = jnp.stack([w1_part] + [shifted(w1_part, "z", s) for s in range(1, zs)])
+    w1_mine = w1_part[None]
+    while w1_mine.shape[0] < zs:
+        step = w1_mine.shape[0]
+        far = lax.ppermute(w1_mine, "z", [(i, i ^ step) for i in range(zs)])
+        w1_mine = jnp.concatenate([w1_mine, far])
     w1_other = swap_core(w1_mine)
     normed = lax.all_to_all(sent, CTX, 0, 0, tiled=True).reshape(blocks, records, local_len, model)
     cat_b = jnp.concatenate([w_proj, w_first], 1)
@@ -525,6 +543,7 @@
     keep, send = call(
         sum_body, [(chunk[1:], BF)] * 2, [scal] + sums, "share_sum", 16, [pltpu.VMEM(chunk, F32)]
     )
+    attn_in, keep, send = barrier((attn_in, keep, send))
     pair = jnp.stack([keep, swap_yh(send)])
 
     back = pl.pallas_call(
@@ -546,13 +565,6 @@
     back = lax.all_to_all(back, CTX, 0, 0, tiled=True).reshape(blocks, rows, 3 * width)
     pair, back = barrier((pair, back))
     pair = lax.all_to_all(jnp.broadcast_to(pair, (blocks,) + chunk), CTX, 0, 0, tiled=True)
-    grad_first, grad_kernel = call(
-        last_body,
-        [((depth, 2 * model), F32), ((taps, model), F32)],
-        [scal, pair],
-        "lay_out",
-        16,
-    )
     result, grad_in = call(
         result_body,
         [((rows, model), BF), ((rows, model), BF)],
@@ -565,6 +577,14 @@
             pltpu.SemaphoreType.DMA((8,)),
         ],
         [all_b, other_b],
+    )
+    pair, result, grad_in = barrier((pair, result, grad_in))
+    grad_first, grad_kernel = call(
+        last_body,
+        [((depth, 2 * model), F32), ((taps, model), F32)],
+        [scal, pair],
+        "lay_out",
+        16,
     )
     return (
         result.reshape(records, local_len, model),

time: 200 us -> 185 us (0.925)
  blocking collectives: 36.2 us -> 23.6 us
  waiting for transfers between devices: 41.9 us -> 35.7 us
  starting transfers between devices: 56.8 us -> 53.5 us
  Pallas kernels: 40.2 us -> 43.4 us
  local copies, waits for them, and re-layouts: 7.45 us -> 9.69 us
    ppermute x14 -> x7, starting transfers between devices: 34.9 us -> 15.2 us  [shifted(): return lax.ppermute(v, axis, [(i, (i + by) % count) for i in range(count)])]
    all_to_all x1, waiting for transfers between devices: 18.5 us -> 0.01 us  [local(): attn_in = lax.all_to_all(sent, CTX, 0, 0, tiled=True)]
    ppermute x0 -> x3, starting transfers between devices: none -> 12.9 us  [local(): far = lax.ppermute(w1_mine, 'z', [(i, i ^ step) for i in range(zs)])]
    all_to_all x1 -> x0, blocking collectives: 12.4 us -> none  [local(): lax.all_to_all(jnp.broadcast_to(pair, (blocks,) + chunk), CTX, 0, 0, tile...]
    ppermute x0 -> x3, waiting for transfers between devices: none -> 12.1 us  [local(): far = lax.ppermute(w1_mine, 'z', [(i, i ^ step) for i in range(zs)])]
    all_to_all x1, waiting for transfers between devices: 9.65 us -> 0.01 us  [local(): lax.all_to_all(sent, CTX, 0, 0, tiled=True)]
    all_to_all x1, waiting for transfers between devices: 0.01 us -> 8.34 us  [local(): lax.all_to_all(back, CTX, 0, 0, tiled=True).reshape(blocks, rows, 3 * width)]
    all_gather x1, waiting for transfers between devices: 0.01 us -> 6.81 us  [local(): all_a = lax.all_gather(shard_a, 'z', axis=0, tiled=False)]
  transfers between devices with their start and end apart: 27 -> 24, of which waited for: 11 -> 11; matrix products, arithmetic and copies ran while one was open for 1% -> 2% of each run, Pallas kernels for 16% -> 22%
where the time goes in v1:
time: 185 us; the launch traced here: 183 us
  starting transfers between devices  53.5 us (29%)
  Pallas kernels  43.4 us (23%)
  waiting for transfers between devices  35.7 us (19%)
  blocking collectives  23.6 us (13%)
  between operations  14.3 us (8%)
  local copies, waits for them, and re-layouts  9.69 us (5%)
  other arithmetic  3.13 us (2%)
    pallas_call x9, Pallas kernels, call(): pl.pallas_call(body, grid=(1,), out_shape=tuple((jax.ShapeDtypeStruct(*o)...  25.2 us
    ppermute x7, starting transfers between devices, shifted(): return lax.ppermute(v, axis, [(i, (i + by) % count) for i in range(count)])  15.2 us
    ppermute x3, starting transfers between devices, local(): far = lax.ppermute(w1_mine, 'z', [(i, i ^ step) for i in range(zs)])  12.9 us
    all_to_all x1, blocking collectives, local(): lax.all_to_all(conv, CTX, 0, 0, tiled=True).reshape(blocks, rows, width)  12.2 us
    ppermute x3, waiting for transfers between devices, local(): far = lax.ppermute(w1_mine, 'z', [(i, i ^ step) for i in range(zs)])  12.1 us
    all_to_all x1, blocking collectives, local(): grad_conv = lax.all_to_all(grad_conv, CTX, 0, 0, tiled=True)  11.4 us
    all_to_all x1, waiting for transfers between devices, local(): lax.all_to_all(back, CTX, 0, 0, tiled=True).reshape(blocks, rows, 3 * width)  8.34 us
    unnamed x45, local copies, waits for them, and re-layouts  8.25 us
  transfers between devices with their start and end apart: 24, of which 11 were waited for; matrix products, arithmetic and copies ran while one was open for 2% of the time, Pallas kernels for 22%

profile of v1, /device:TPU:8, one launch (start us, length us, event | category | flops | bytes accessed | tf_op | source)
XLA Modules:
  0.0 183.2 jit_solution(13411445208755996384)
XLA Ops:
  10.5 2.6 %first_norm.1 = bf16[8,128,1024]{2,1,0:T(8,128)(2,1)} custom-call(s32[2]{0:T(128)} %scal.23, bf16[128,1024]{1,0:T(8,128)(2,1)} %bitcast.27, f32[1,1024]{1,0:T(1,128)} %bitcast.42), custom_call_target="tpu_custom_call" | custom-call | tf_op jit(solution)/shard_map/first_norm/pallas_call | solution.py:63
  13.1 6.2 %all-to-all-start = ((bf16[8,128,1024]{2,1,0:T(8,128)(2,1)}), bf16[8,128,1024]{2,1,0:T(8,128)(2,1)S(1)}, u32[]{:S(2)}, u32[]{:S(2)}) async-start(bf16[8,128,1024]{2,1,0:T(8,128)(2,1)} %first_norm.1), calls=%async_computation | async-start | bytes 4194304 | tf_op jit(solution)/shard_map/all_to_all | solution.py:450
  25.2 2.2 %collective-permute-done.1 = bf16[1,2,32,256]{3,2,1,0:T(8,128)(2,1)S(1)} collective-permute-done((bf16[1,2,32,256]{3,2,1,0:T(8,128)(2,1)}, bf16[1,2,32,256]{3,2,1,0:T(8,128)(2,1)S(1)}, u32[]{:S(2)}, u32[]{:S(2)}) %collective-permute-start.1) | collective-permute-done | bytes 32800 | tf_op jit(solution)/shard_map/ppermute | solution.py:447
  28.2 3.3 %collective-permute-start.2 = (bf16[2,2,32,256]{3,2,1,0:T(8,128)(2,1)S(1)}, bf16[2,2,32,256]{3,2,1,0:T(8,128)(2,1)S(1)}, u32[]{:S(2)}, u32[]{:S(2)}) collective-permute-start(bf16[2,2,32,256]{3,2,1,0:T(8,128)(2,1)S(1)} %pad_maximum_fusion.3), channel_id=1, source_target_pairs={{0,32},{16,48},{32,0},{48,16},{64,96},{80,112},{96,64},{112,80},{1... | collective-permute-start | bytes 196616 | tf_op jit(solution)/shard_map/ppermute | solution.py:447
  31.5 2.2 %collective-permute-done.2 = bf16[2,2,32,256]{3,2,1,0:T(8,128)(2,1)S(1)} collective-permute-done((bf16[2,2,32,256]{3,2,1,0:T(8,128)(2,1)S(1)}, bf16[2,2,32,256]{3,2,1,0:T(8,128)(2,1)S(1)}, u32[]{:S(2)}, u32[]{:S(2)}) %collective-permute-start.2) | collective-permute-done | bytes 65568 | tf_op jit(solution)/shard_map/ppermute | solution.py:447
  34.5 7.7 %collective-permute-start.3 = (bf16[4,2,32,256]{3,2,1,0:T(8,128)(2,1)S(1)}, bf16[4,2,32,256]{3,2,1,0:T(8,128)(2,1)S(1)}, u32[]{:S(2)}, u32[]{:S(2)}) collective-permute-start(bf16[4,2,32,256]{3,2,1,0:T(8,128)(2,1)S(1)} %pad_maximum_fusion.2), channel_id=1, source_target_pairs={{0,64},{16,80},{32,96},{48,112},{64,0},{80,16},{96,32},{112,48},{1... | collective-permute-start | bytes 393224 | tf_op jit(solution)/shard_map/ppermute | solution.py:447
  43.0 7.7 %collective-permute-done.3 = bf16[4,2,32,256]{3,2,1,0:T(8,128)(2,1)S(1)} collective-permute-done((bf16[4,2,32,256]{3,2,1,0:T(8,128)(2,1)S(1)}, bf16[4,2,32,256]{3,2,1,0:T(8,128)(2,1)S(1)}, u32[]{:S(2)}, u32[]{:S(2)}) %collective-permute-start.3) | collective-permute-done | bytes 131104 | tf_op jit(solution)/shard_map/ppermute | solution.py:447
  54.5 4.4 %gate_conv.1 = (bf16[8,2,64,128]{3,2,1,0:T(8,128)(2,1)}, f32[2,512,256]{2,1,0:T(8,128)}, bf16[2,512,128]{2,1,0:T(8,128)(2,1)}) custom-call(s32[2]{0:T(128)} %scal.23, bf16[8,2,64,1024]{3,2,1,0:T(8,128)(2,1)} %bitcast.19, bf16[8,2,32,256]{3,2,1,0:T(8,128)(2,1)} %copy-done.5, bf16[8,2,32,256]{3,2,1,0:T(8,128)(2,1)} %copy-done.7, ...), custom_call_target="tpu_custom_call" | custom-call | tf_op jit(solution)/shard_map/gate_conv/pallas_call | solution.py:458
  58.9 6.8 %all-gather.5.cloned.1.call-done = bf16[16,32,1408]{2,1,0:T(8,128)(2,1)} async-done(((bf16[2,32,1408]{2,1,0:T(8,128)(2,1)}), bf16[16,32,1408]{2,1,0:T(8,128)(2,1)}) %all-gather.5.cloned.1.call-update) | async-done | bytes 1441808 | tf_op jit(solution)/shard_map/all_gather | solution.py:443
  65.8 12.2 %all_to_all.30 = bf16[8,2,64,128]{3,2,1,0:T(8,128)(2,1)} all-to-all(bf16[8,2,64,128]{3,2,1,0:T(8,128)(2,1)} %get-tuple-element.51), channel_id=1, replica_groups=mesh['yh'=2,'z'=8,'core'=2,'yl'=2,'x'=4] {'yl','x'}, dimensions={0} | all-to-all | bytes 524288 | tf_op jit(solution)/shard_map/all_to_all | solution.py:486
  79.1 5.6 %token_rows.1 = (bf16[8,128,1024]{2,1,0:T(8,128)(2,1)}, bf16[128,1024]{1,0:T(8,128)(2,1)}, bf16[8,128,128]{2,1,0:T(8,128)(2,1)}) custom-call(s32[2]{0:T(128)} %scal.23, bf16[8,128,128]{2,1,0:T(8,128)(2,1)} %bitcast.33, bf16[128,1024]{1,0:T(8,128)(2,1)} %bitcast.28, bf16[128,1024]{1,0:T(8,128)(2,1)} %bitcast.30, f32[1,1024]{1,0:T(1,128)} %bitcast.44, ...), custom_call_target="tpu_custom_call" | custom-call | tf_op jit(solution)/shard_map/token_rows/pallas_call | solution.py:63
  84.7 11.4 %all_to_all.31 = bf16[8,128,128]{2,1,0:T(8,128)(2,1)} all-to-all(bf16[8,128,128]{2,1,0:T(8,128)(2,1)} %get-tuple-element.55), channel_id=1, replica_groups=mesh['yh'=2,'z'=8,'core'=2,'yl'=2,'x'=4] {'yl','x'}, dimensions={0} | all-to-all | bytes 524288 | tf_op jit(solution)/shard_map/all_to_all | solution.py:500
  96.1 5.0 %all-to-all-start.3 = ((bf16[8,128,1024]{2,1,0:T(8,128)(2,1)}), bf16[8,128,1024]{2,1,0:T(8,128)(2,1)S(1)}, u32[]{:S(2)}, u32[]{:S(2)}) async-start(bf16[8,128,1024]{2,1,0:T(8,128)(2,1)} %get-tuple-element.56), calls=%async_computation.3 | async-start | bytes 4194304 | tf_op jit(solution)/shard_map/all_to_all | solution.py:504
  101.1 6.3 %conv_back.1 = (bf16[8,2,64,256]{3,2,1,0:T(8,128)(2,1)}, f32[2,8,32,256]{3,2,1,0:T(8,128)}, bf16[2,8,32,256]{3,2,1,0:T(8,128)(2,1)}, f32[16,256]{1,0:T(8,128)}) custom-call(s32[2]{0:T(128)} %scal.23, bf16[8,2,64,128]{3,2,1,0:T(8,128)(2,1)} %bitcast.32, f32[2,512,256]{2,1,0:T(8,128)} %get-tuple-element.58.hid_ref, ...), custom_call_target="tpu_custom_call" | custom-call | tf_op jit(solution)/shard_map/conv_back/pallas_call | solution.py:509
  111.9 2.3 %collective-permute-start.10 = (bf16[2,48,256]{2,1,0:T(8,128)(2,1)}, bf16[2,48,256]{2,1,0:T(8,128)(2,1)S(1)}, u32[]{:S(2)}, u32[]{:S(2)}) collective-permute-start(bf16[2,48,256]{2,1,0:T(8,128)(2,1)} %get-tuple-element.65), channel_id=1, source_target_pairs={{0,32},{16,48},{32,64},{48,80},{64,96},{80,112},{96,0},{112,16},{1... | collective-permute-start | bytes 147464 | tf_op jit(solution)/shard_map/ppermute | solution.py:384
  116.1 3.4 %collective-permute-start.12 = (bf16[2,48,256]{2,1,0:T(8,128)(2,1)}, bf16[2,48,256]{2,1,0:T(8,128)(2,1)S(1)}, u32[]{:S(2)}, u32[]{:S(2)}) collective-permute-start(bf16[2,48,256]{2,1,0:T(8,128)(2,1)} %get-tuple-element.67), channel_id=1, source_target_pairs={{0,64},{16,80},{32,96},{48,112},{64,0},{80,16},{96,32},{112,48},{1... | collective-permute-start | bytes 147464 | tf_op jit(solution)/shard_map/ppermute | solution.py:384
  119.5 2.2 %collective-permute-start.13 = (bf16[2,48,256]{2,1,0:T(8,128)(2,1)}, bf16[2,48,256]{2,1,0:T(8,128)(2,1)S(1)}, u32[]{:S(2)}, u32[]{:S(2)}) collective-permute-start(bf16[2,48,256]{2,1,0:T(8,128)(2,1)} %get-tuple-element.68), channel_id=1, source_target_pairs={{0,80},{16,96},{32,112},{48,0},{64,16},{80,32},{96,48},{112,64},{1... | collective-permute-start | bytes 147464 | tf_op jit(solution)/shard_map/ppermute | solution.py:384
  121.8 3.3 %collective-permute-start.14 = (bf16[2,48,256]{2,1,0:T(8,128)(2,1)}, bf16[2,48,256]{2,1,0:T(8,128)(2,1)S(1)}, u32[]{:S(2)}, u32[]{:S(2)}) collective-permute-start(bf16[2,48,256]{2,1,0:T(8,128)(2,1)} %get-tuple-element.69), channel_id=1, source_target_pairs={{0,96},{16,112},{32,0},{48,16},{64,32},{80,48},{96,64},{112,80},{1... | collective-permute-start | bytes 147464 | tf_op jit(solution)/shard_map/ppermute | solution.py:384
  134.3 7.5 %heads.1 = bf16[8,2,64,384]{3,2,1,0:T(8,128)(2,1)} custom-call(s32[2]{0:T(128)} %scal.23, bf16[8,2,64,1024]{3,2,1,0:T(8,128)(2,1)} %bitcast.21, bf16[8,2,64,256]{3,2,1,0:T(8,128)(2,1)} %get-tuple-element.77.gh_ref, bf16[8,2,32,1408]{3,2,1,0:T(8,128)(2,1)} %bitcast.24, bf16[8,2,32,1408]{3,2,1,0:T(8,128)(2,1)} %copy-done.2), custom_call_target="tpu_custom_call" | custom-call | tf_op jit(solution)/shard_map/heads/pallas_call | solution.py:549
  141.9 5.7 %all-to-all-start.4 = ((bf16[8,2,64,384]{3,2,1,0:T(8,128)(2,1)}), bf16[8,2,64,384]{3,2,1,0:T(8,128)(2,1)}, u32[]{:S(2)}, u32[]{:S(2)}) async-start(bf16[8,2,64,384]{3,2,1,0:T(8,128)(2,1)} %heads.1), calls=%async_computation.4 | async-start | bytes 1572864 | tf_op jit(solution)/shard_map/all_to_all | solution.py:565
  148.7 2.8 %collective-permute-done.16 = bf16[48,256]{1,0:T(8,128)(2,1)S(1)} collective-permute-done((bf16[48,256]{1,0:T(8,128)(2,1)S(1)}, bf16[48,256]{1,0:T(8,128)(2,1)S(1)}, u32[]{:S(2)}, u32[]{:S(2)}) %collective-permute-start.16) | collective-permute-done | bytes 24608 | tf_op jit(solution)/shard_map/ppermute | solution.py:379
  151.5 8.3 %all-to-all-done.4 = bf16[8,2,64,384]{3,2,1,0:T(8,128)(2,1)} async-done(((bf16[8,2,64,384]{3,2,1,0:T(8,128)(2,1)}), bf16[8,2,64,384]{3,2,1,0:T(8,128)(2,1)}, u32[]{:S(2)}, u32[]{:S(2)}) %all-to-all-start.4) | async-done | bytes 786464 | tf_op jit(solution)/shard_map/all_to_all | solution.py:565
  160.7 4.8 %all-to-all-start.5 = ((bf16[8,2,48,256]{3,2,1,0:T(8,128)(2,1)}), bf16[8,2,48,256]{3,2,1,0:T(8,128)(2,1)S(1)}, u32[]{:S(2)}, u32[]{:S(2)}) async-start(bf16[8,2,48,256]{3,2,1,0:T(8,128)(2,1)} %broadcast_in_dim.7), calls=%async_computation.5 | async-start | bytes 786432 | tf_op jit(solution)/shard_map/all_to_all | solution.py:567
  167.2 6.6 %result_rows.1 = (bf16[128,1024]{1,0:T(8,128)(2,1)}, bf16[128,1024]{1,0:T(8,128)(2,1)}) custom-call(s32[2]{0:T(128)} %scal.23, bf16[8,128,384]{2,1,0:T(8,128)(2,1)} %bitcast.16.a_ref, bf16[128,1024]{1,0:T(8,128)(2,1)} %get-tuple-element.81.res_ref, bf16[128,1024]{1,0:T(8,128)(2,1)} %bitcast.29, bf16[128,1024]{1,0:T(8,128)(2,1)} %bitcast.31, ...), custom_call_target="tpu_custom_call" | custom-call | tf_op jit(solution)/shard_map/result_rows/pallas_call | solution.py:63
  (93 shorter events, 38.3 us)
Async XLA Ops:
  8.9 10.4 %collective-permute-start = (bf16[32,1664]{1,0:T(8,128)(2,1)}, bf16[32,1664]{1,0:T(8,128)(2,1)S(1)}, u32[]{:S(2)}, u32[]{:S(2)}) collective-permute-start(bf16[32,1664]{1,0:T(8,128)(2,1)} %get-tuple-element.48), channel_id=1, source_target_pairs={{0,132},{132,0},{4,128},{128,4},{1,133},{133,1},{5,129},{129,5},{2... | collective-permute-start | bytes 319496 | tf_op jit(solution)/shard_map/ppermute | solution.py:379
  13.1 40.0 %all-to-all-start = ((bf16[8,128,1024]{2,1,0:T(8,128)(2,1)}), bf16[8,128,1024]{2,1,0:T(8,128)(2,1)S(1)}, u32[]{:S(2)}, u32[]{:S(2)}) async-start(bf16[8,128,1024]{2,1,0:T(8,128)(2,1)} %first_norm.1), calls=%async_computation | async-start | bytes 4194304 | tf_op jit(solution)/shard_map/all_to_all | solution.py:450
  19.3 46.4 %all-gather.5.cloned.1.call-start = ((), (), s32[]{:S(2)}) async-start(), calls=%async_computation.6 | async-start | bytes 1622016 | tf_op jit(solution)/shard_map/all_gather | solution.py:443
  21.6 120.2 %all-gather.7.cloned.1.call-start = ((), (), s32[]{:S(2)}) async-start(), calls=%async_computation.7 | async-start | bytes 3538944 | tf_op jit(solution)/shard_map/all_gather | solution.py:485
  23.3 4.1 %collective-permute-start.1 = (bf16[1,2,32,256]{3,2,1,0:T(8,128)(2,1)}, bf16[1,2,32,256]{3,2,1,0:T(8,128)(2,1)S(1)}, u32[]{:S(2)}, u32[]{:S(2)}) collective-permute-start(bf16[1,2,32,256]{3,2,1,0:T(8,128)(2,1)} %bitcast.35), channel_id=1, source_target_pairs={{0,16},{16,0},{32,48},{48,32},{64,80},{80,64},{96,112},{112,96},{1... | collective-permute-start | bytes 98312 | tf_op jit(solution)/shard_map/ppermute | solution.py:447
  28.2 5.5 %collective-permute-start.2 = (bf16[2,2,32,256]{3,2,1,0:T(8,128)(2,1)S(1)}, bf16[2,2,32,256]{3,2,1,0:T(8,128)(2,1)S(1)}, u32[]{:S(2)}, u32[]{:S(2)}) collective-permute-start(bf16[2,2,32,256]{3,2,1,0:T(8,128)(2,1)S(1)} %pad_maximum_fusion.3), channel_id=1, source_target_pairs={{0,32},{16,48},{32,0},{48,16},{64,96},{80,112},{96,64},{112,80},{1... | collective-permute-start | bytes 196616 | tf_op jit(solution)/shard_map/ppermute | solution.py:447
  34.5 16.2 %collective-permute-start.3 = (bf16[4,2,32,256]{3,2,1,0:T(8,128)(2,1)S(1)}, bf16[4,2,32,256]{3,2,1,0:T(8,128)(2,1)S(1)}, u32[]{:S(2)}, u32[]{:S(2)}) collective-permute-start(bf16[4,2,32,256]{3,2,1,0:T(8,128)(2,1)S(1)} %pad_maximum_fusion.2), channel_id=1, source_target_pairs={{0,64},{16,80},{32,96},{48,112},{64,0},{80,16},{96,32},{112,48},{1... | collective-permute-start | bytes 393224 | tf_op jit(solution)/shard_map/ppermute | solution.py:447
  42.2 9.3 %collective-permute-start.5 = (bf16[32,3072]{1,0:T(8,128)(2,1)S(1)}, bf16[32,3072]{1,0:T(8,128)(2,1)S(1)}, u32[]{:S(2)}, u32[]{:S(2)}) collective-permute-start(bf16[32,3072]{1,0:T(8,128)(2,1)S(1)} %constant_dynamic-update-slice_fusion), channel_id=1, source_target_pairs={{0,132},{132,0},{4,128},{128,4},{1,133},{133,1},{5,129},{129,5},{2... | collective-permute-start | bytes 589832 | tf_op jit(solution)/shard_map/ppermute | solution.py:379
  51.5 1.6 collective-permute-start.4
  65.7 12.3 %collective-permute-start.6 = (bf16[8,2,32,1408]{3,2,1,0:T(8,128)(2,1)}, bf16[8,2,32,1408]{3,2,1,0:T(8,128)(2,1)S(1)}, u32[]{:S(2)}, u32[]{:S(2)}) collective-permute-start(bf16[8,2,32,1408]{3,2,1,0:T(8,128)(2,1)} %bitcast.22), channel_id=1, source_target_pairs={{0,8},{8,0},{1,9},{9,1},{2,10},{10,2},{3,11},{11,3},{4,12},{12,4},... | collective-permute-start | bytes 4325384 | tf_op jit(solution)/shard_map/ppermute | solution.py:375
  96.1 36.8 %all-to-all-start.3 = ((bf16[8,128,1024]{2,1,0:T(8,128)(2,1)}), bf16[8,128,1024]{2,1,0:T(8,128)(2,1)S(1)}, u32[]{:S(2)}, u32[]{:S(2)}) async-start(bf16[8,128,1024]{2,1,0:T(8,128)(2,1)} %get-tuple-element.56), calls=%async_computation.3 | async-start | bytes 4194304 | tf_op jit(solution)/shard_map/all_to_all | solution.py:504
  107.4 1.9 %collective-permute-start.7 = (bf16[2,8,32,256]{3,2,1,0:T(8,128)(2,1)}, bf16[2,8,32,256]{3,2,1,0:T(8,128)(2,1)S(1)}, u32[]{:S(2)}, u32[]{:S(2)}) collective-permute-start(bf16[2,8,32,256]{3,2,1,0:T(8,128)(2,1)} %get-tuple-element.61), channel_id=1, source_target_pairs={{0,8},{8,0},{1,9},{9,1},{2,10},{10,2},{3,11},{11,3},{4,12},{12,4},... | collective-permute-start | bytes 786440 | tf_op jit(solution)/shard_map/ppermute | solution.py:375
  107.5 1.8 collective-permute-start.8
  111.9 13.2 %collective-permute-start.10 = (bf16[2,48,256]{2,1,0:T(8,128)(2,1)}, bf16[2,48,256]{2,1,0:T(8,128)(2,1)S(1)}, u32[]{:S(2)}, u32[]{:S(2)}) collective-permute-start(bf16[2,48,256]{2,1,0:T(8,128)(2,1)} %get-tuple-element.65), channel_id=1, source_target_pairs={{0,32},{16,48},{32,64},{48,80},{64,96},{80,112},{96,0},{112,16},{1... | collective-permute-start | bytes 147464 | tf_op jit(solution)/shard_map/ppermute | solution.py:384
  114.2 11.0 %collective-permute-start.11 = (bf16[2,48,256]{2,1,0:T(8,128)(2,1)}, bf16[2,48,256]{2,1,0:T(8,128)(2,1)S(1)}, u32[]{:S(2)}, u32[]{:S(2)}) collective-permute-start(bf16[2,48,256]{2,1,0:T(8,128)(2,1)} %get-tuple-element.66), channel_id=1, source_target_pairs={{0,48},{16,64},{32,80},{48,96},{64,112},{80,0},{96,16},{112,32},{1... | collective-permute-start | bytes 147464 | tf_op jit(solution)/shard_map/ppermute | solution.py:384
  116.1 11.0 %collective-permute-start.12 = (bf16[2,48,256]{2,1,0:T(8,128)(2,1)}, bf16[2,48,256]{2,1,0:T(8,128)(2,1)S(1)}, u32[]{:S(2)}, u32[]{:S(2)}) collective-permute-start(bf16[2,48,256]{2,1,0:T(8,128)(2,1)} %get-tuple-element.67), channel_id=1, source_target_pairs={{0,64},{16,80},{32,96},{48,112},{64,0},{80,16},{96,32},{112,48},{1... | collective-permute-start | bytes 147464 | tf_op jit(solution)/shard_map/ppermute | solution.py:384
  119.5 8.6 %collective-permute-start.13 = (bf16[2,48,256]{2,1,0:T(8,128)(2,1)}, bf16[2,48,256]{2,1,0:T(8,128)(2,1)S(1)}, u32[]{:S(2)}, u32[]{:S(2)}) collective-permute-start(bf16[2,48,256]{2,1,0:T(8,128)(2,1)} %get-tuple-element.68), channel_id=1, source_target_pairs={{0,80},{16,96},{32,112},{48,0},{64,16},{80,32},{96,48},{112,64},{1... | collective-permute-start | bytes 147464 | tf_op jit(solution)/shard_map/ppermute | solution.py:384
  121.8 8.4 %collective-permute-start.14 = (bf16[2,48,256]{2,1,0:T(8,128)(2,1)}, bf16[2,48,256]{2,1,0:T(8,128)(2,1)S(1)}, u32[]{:S(2)}, u32[]{:S(2)}) collective-permute-start(bf16[2,48,256]{2,1,0:T(8,128)(2,1)} %get-tuple-element.69), channel_id=1, source_target_pairs={{0,96},{16,112},{32,0},{48,16},{64,32},{80,48},{96,64},{112,80},{1... | collective-permute-start | bytes 147464 | tf_op jit(solution)/shard_map/ppermute | solution.py:384
  125.1 5.6 %collective-permute-start.15 = (bf16[2,48,256]{2,1,0:T(8,128)(2,1)}, bf16[2,48,256]{2,1,0:T(8,128)(2,1)S(1)}, u32[]{:S(2)}, u32[]{:S(2)}) collective-permute-start(bf16[2,48,256]{2,1,0:T(8,128)(2,1)} %get-tuple-element.70), channel_id=1, source_target_pairs={{0,112},{16,0},{32,16},{48,32},{64,48},{80,64},{96,80},{112,96},{1... | collective-permute-start | bytes 147464 | tf_op jit(solution)/shard_map/ppermute | solution.py:384
  125.2 5.5 %collective-permute-start.9 = (bf16[2,48,256]{2,1,0:T(8,128)(2,1)}, bf16[2,48,256]{2,1,0:T(8,128)(2,1)S(1)}, u32[]{:S(2)}, u32[]{:S(2)}) collective-permute-start(bf16[2,48,256]{2,1,0:T(8,128)(2,1)} %get-tuple-element.64), channel_id=1, source_target_pairs={{0,16},{16,32},{32,48},{48,64},{64,80},{80,96},{96,112},{112,0},{1... | collective-permute-start | bytes 147464 | tf_op jit(solution)/shard_map/ppermute | solution.py:384
  141.8 23.7 %collective-permute-start.17 = (bf16[8,2,32,3072]{3,2,1,0:T(8,128)(2,1)}, bf16[8,2,32,3072]{3,2,1,0:T(8,128)(2,1)S(1)}, u32[]{:S(2)}, u32[]{:S(2)}) collective-permute-start(bf16[8,2,32,3072]{3,2,1,0:T(8,128)(2,1)} %bitcast.25), channel_id=1, source_target_pairs={{0,8},{8,0},{1,9},{9,1},{2,10},{10,2},{3,11},{11,3},{4,12},{12,4},... | collective-permute-start | bytes 9437192 | tf_op jit(solution)/shard_map/ppermute | solution.py:375
  141.9 17.9 %all-to-all-start.4 = ((bf16[8,2,64,384]{3,2,1,0:T(8,128)(2,1)}), bf16[8,2,64,384]{3,2,1,0:T(8,128)(2,1)}, u32[]{:S(2)}, u32[]{:S(2)}) async-start(bf16[8,2,64,384]{3,2,1,0:T(8,128)(2,1)} %heads.1), calls=%async_computation.4 | async-start | bytes 1572864 | tf_op jit(solution)/shard_map/all_to_all | solution.py:565
  147.7 3.8 %collective-permute-start.16 = (bf16[48,256]{1,0:T(8,128)(2,1)S(1)}, bf16[48,256]{1,0:T(8,128)(2,1)S(1)}, u32[]{:S(2)}, u32[]{:S(2)}) collective-permute-start(bf16[48,256]{1,0:T(8,128)(2,1)S(1)} %copy-done.21), channel_id=1, source_target_pairs={{0,132},{132,0},{4,128},{128,4},{1,133},{133,1},{5,129},{129,5},{2... | collective-permute-start | bytes 73736 | tf_op jit(solution)/shard_map/ppermute | solution.py:379
  160.7 13.2 %all-to-all-start.5 = ((bf16[8,2,48,256]{3,2,1,0:T(8,128)(2,1)}), bf16[8,2,48,256]{3,2,1,0:T(8,128)(2,1)S(1)}, u32[]{:S(2)}, u32[]{:S(2)}) async-start(bf16[8,2,48,256]{3,2,1,0:T(8,128)(2,1)} %broadcast_in_dim.7), calls=%async_computation.5 | async-start | bytes 786432 | tf_op jit(solution)/shard_map/all_to_all | solution.py:567
  (22 other events, 111.3 us)
Sparse Core Ops, SparseCore 0:
  21.9 43.7 all-gather.4
  67.5 44.2 all-gather.6
